TPU v7x, 512 devices: a whole 4x4x16 slice. The times are simulated.
512 devices in a mesh: dp: 64 (over x, z), tp: 8 (over y, core).
Axes of the slice: x: 4, y: 4, z: 16, core: 2. Of those that a mesh axis runs over, the one named last changes fastest.
Arguments:
- layer_input: bfloat16 [65536, 2560], P(('dp', 'tp')), may hold values from -6 to 6
- queries: bfloat16 [65536, 3072], P('dp', 'tp'), may hold values from -6 to 6
- key_vectors: bfloat16 [65536, 3072], P('dp', 'tp'), may hold values from -6 to 6
- out_grad: bfloat16 [65536, 3072], P('dp', 'tp'), may hold values from -6 to 6
- feedback: bfloat16 [163840, 3072], P('dp', 'tp'), may hold values from -48 to 48
- factor_prev: float32 [32, 3072], P(None, 'tp'), may hold values from -6 to 6
- token_count: int32 [64], P('dp'), may hold values from 204 to 1024, as said below
- segment_ids: int32 [65536], P('dp'), may hold values from 0 to 32, as said below
Outputs:
- basis: float32 [32, 2560], P(None, 'tp')
- factor_next: float32 [32, 3072], P(None, 'tp')
Inputs may be any that keep to these rules, and one draw needn't show every extreme that they name: `token_count`: the number of real tokens of each replica's buffer of 1024 slots; later slots are padding; some replica is full. `segment_ids`: within each replica's 1024 slots the ids start at 0 and never fall, rising by at most one a slot; the first 16 slots of a replica share id 0; every replica holds exactly 33 documents.
All inputs are finite; a program needn't handle non-finite values.
Results may differ from a plain program's by a relative error of at most 0.0042.
Values may be sent and summed in bfloat16 or wider, within the bound.
A program may use at most 64 MiB of HBM per device.

v0:
```python
import functools
import math

import jax
import jax.numpy as jnp
from jax import lax
from jax.sharding import PartitionSpec as P

HEAD_DIM = 128


masked_score = -1e30


def block_values(
    query_heads, key_heads, grad_heads, segment_ids, positions, live_count, first_row, last_row
):
    scaling = HEAD_DIM ** (-0.5)
    scores = (
        jnp.einsum(
            "qhd,khd->hqk",
            query_heads[first_row:last_row],
            key_heads[:last_row],
            preferred_element_type=jnp.float32,
        )
        * scaling
    )
    query_pos = positions[first_row:last_row]
    key_pos = positions[:last_row]
    allowed = (
        (segment_ids[first_row:last_row, None] == segment_ids[None, :last_row])
        & (key_pos[None, :] <= query_pos[:, None])
        & (query_pos[:, None] < live_count)
        & (key_pos[None, :] < live_count)
    )
    masked = jnp.where(allowed[None], scores, masked_score)
    highest = jnp.max(masked, axis=-1, keepdims=True)
    raised = jnp.where(allowed[None], jnp.exp(masked - highest), 0.0)
    totals = jnp.maximum(jnp.sum(raised, axis=-1, keepdims=True), 1.0)
    weights = (raised / totals).astype(jnp.bfloat16)
    return jnp.einsum(
        "hqk,qhd->khd", weights, grad_heads[first_row:last_row], preferred_element_type=jnp.float32
    )


def value_grads(queries, key_vectors, out_grad, live_count, segment_ids):
    length = queries.shape[0]
    head_count = queries.shape[1] // HEAD_DIM
    query_heads = queries.reshape(length, head_count, HEAD_DIM)
    key_heads = key_vectors.reshape(length, head_count, HEAD_DIM)
    grad_heads = out_grad.reshape(length, head_count, HEAD_DIM)
    positions = jnp.arange(length, dtype=jnp.int32)
    block_size = min(512, length)
    summed = jnp.zeros((length, head_count, HEAD_DIM), jnp.float32)
    for number in range(length // block_size):
        first_row = number * block_size
        last_row = first_row + block_size
        compute = functools.partial(
            block_values,
            query_heads,
            key_heads,
            grad_heads,
            segment_ids,
            positions,
            live_count,
            first_row,
            last_row,
        )
        portion = compute()
        summed = summed.at[:last_row].add(portion)
    return summed.reshape(length, -1).astype(jnp.bfloat16)


def on_device(
    layer_input, queries, key_vectors, out_grad, feedback, factor_prev, token_count, segment_ids
):
    precise = lax.Precision.HIGHEST
    live_count = token_count[0]
    values = value_grads(queries, key_vectors, out_grad, live_count, segment_ids)
    carried = feedback.astype(jnp.float32)
    gradient = lax.dot_general(
        lax.all_gather(layer_input, "tp", axis=0, tiled=True),
        values,
        (((0,), (0,)), ((), ())),
        preferred_element_type=jnp.float32,
    )
    matrix = gradient + carried
    left_term = lax.dot_general(factor_prev, matrix, (((1,), (1,)), ((), ())), precision=precise)
    width_share = layer_input.shape[1] // lax.axis_size("tp")
    left_all = lax.psum(left_term, ("dp", "tp"))
    gram_matrix = jnp.dot(left_all, left_all.T, precision=precise)
    cholesky_low = jnp.linalg.cholesky(gram_matrix)
    basis_full = lax.linalg.triangular_solve(cholesky_low, left_all, left_side=True, lower=True)
    basis_own = lax.dynamic_slice_in_dim(
        basis_full, lax.axis_index("tp") * width_share, width_share, 1
    )
    right_term = jnp.dot(basis_full, matrix, precision=precise)
    factor_next = lax.psum(right_term, "dp") / lax.axis_size("dp")
    return (basis_own * math.sqrt(layer_input.shape[1]), factor_next)


def solution(mesh):
    return jax.shard_map(
        on_device,
        mesh=mesh,
        in_specs=(
            P(("dp", "tp"), None),
            P("dp", "tp"),
            P("dp", "tp"),
            P("dp", "tp"),
            P("dp", "tp"),
            P(None, "tp"),
            P("dp"),
            P("dp"),
        ),
        out_specs=(P(None, "tp"), P(None, "tp")),
        check_vma=False,
    )
```

profile of v0, /device:TPU:8, one launch (start us, length us, event | category | flops | bytes accessed | tf_op | source)
XLA Modules:
  0.0 828.1 jit_solution(1245592945950782716)
XLA Ops:
  7.2 0.0 copy-start
  7.2 0.0 all-gather.2.cloned.1.call-start
  7.2 0.7 all-gather.2.cloned.1.call-update
  7.9 0.0 all-reduce.3.cloned.1.call-start
  8.6 1.2 fusion.30
  9.8 0.9 copy.34
  10.8 0.0 copy-start.2
  10.8 1.5 copy.17
  12.3 0.8 slice.112
  13.1 2.1 fusion.31
  15.2 0.0 copy-start.6
  15.2 1.9 copy.20
  17.1 0.9 copy.35
  18.0 1.2 copy.26
  19.2 0.0 copy-done.2
  19.2 2.4 copy.27
  21.7 0.0 copy-done.6
  21.7 0.3 and_and_fusion
  22.1 0.0 copy-start.5
  22.1 4.5 fusion.33
  26.5 0.7 fusion.13
  27.3 0.0 copy-done.5
  27.3 0.0 copy-start.4
  27.3 5.6 fusion.34
  32.9 0.0 copy-done.4
  32.9 2.8 fusion.19
  35.8 1.1 copy-done.7
  36.9 0.8 fusion.14
  37.7 20.1 %all-gather.2.cloned.1.call-done = bf16[1024,2560]{1,0:T(8,128)(2,1)} async-done(((bf16[128,2560]{1,0:T(8,128)(2,1)}), bf16[1024,2560]{1,0:T(8,128)(2,1)}) %all-gather.2.cloned.1.call-update) | async-done | bytes 5242896 | tf_op jit(solution)/shard_map/all_gather | solution.py:82
  57.8 0.0 copy-done.3
  57.8 4.7 fusion.3
  62.5 0.0 copy-start.1
  62.5 1.9 copy-done.1
  64.4 0.0 copy-done
  64.4 3.1 convolution_bitcast_fusion.1
  67.5 0.0 all-reduce.3.cloned.1.call-update
  67.5 461.0 %all-reduce.3.cloned.1.call-done = f32[32,2560]{1,0:T(8,128)} async-done(((f32[32,2560]{1,0:T(8,128)}), f32[32,2560]{1,0:T(8,128)}) %all-reduce.3.cloned.1.call-update) | async-done | bytes 327696 | tf_op jit(solution)/shard_map/psum | solution.py:90
  528.5 1.5 fusion.35
  530.0 0.1 copy.28
  530.1 2.9 cholesky.16
  533.0 0.6 compare_reduce_fusion
  533.7 0.7 fusion.22
  534.3 2.4 custom-call.6
  536.8 1.5 fusion.23
  538.2 5.9 fusion.36
  544.1 275.9 %psum.15 = f32[32,384]{1,0:T(8,128)S(1)} all-reduce(f32[32,384]{1,0:T(8,128)S(1)} %fusion.36), channel_id=1, replica_groups=mesh['dp'=64,'tp'=8] {'dp'}, use_global_device_ids=true, to_apply=%region_7.8 | all-reduce | flops 12288 | bytes 98304 | tf_op jit(solution)/shard_map/psum | solution.py:98
  820.0 0.6 broadcast_multiply_fusion
  820.6 0.7 dynamic-slice_multiply_fusion
  (13 shorter events, 0.1 us)
Async XLA Ops:
  7.2 57.2 %copy-start = (f32[32,384]{1,0:T(8,128)S(1)}, f32[32,384]{1,0:T(8,128)}, u32[]{:S(2)}) copy-start(f32[32,384]{1,0:T(8,128)} %param.19) | copy-start | bytes 147460
  7.2 50.6 %all-gather.2.cloned.1.call-start = ((), (), s32[]{:S(2)}) async-start(), calls=%async_computation | async-start | bytes 5898240 | tf_op jit(solution)/shard_map/all_gather | solution.py:82
  7.9 520.6 %all-reduce.3.cloned.1.call-start = ((), (), s32[]{:S(2)}) async-start(), calls=%async_computation.1 | async-start | bytes 655360 | tf_op jit(solution)/shard_map/psum | solution.py:90
  10.8 8.5 %copy-start.2 = (bf16[2560,384]{1,0:T(8,128)(2,1)S(1)}, bf16[2560,384]{1,0:T(8,128)(2,1)}, u32[]{:S(2)}) copy-start(bf16[2560,384]{1,0:T(8,128)(2,1)} %param.18) | copy-start | bytes 5898244
  15.2 6.5 copy-start.6
  22.1 5.2 copy-start.5
  27.3 5.6 copy-start.4
  32.9 4.0 copy-start.7
  36.9 20.9 %copy-start.3 = (bf16[2560,384]{0,1:T(8,128)(2,1)S(1)}, bf16[2560,384]{0,1:T(8,128)(2,1)}, u32[]{:S(2)}) copy-start(bf16[2560,384]{0,1:T(8,128)(2,1)} %copy.27) | copy-start | bytes 5898244
  62.5 1.9 copy-start.1
Sparse Core Ops, SparseCore 0:
  10.1 47.6 all-gather.1
  67.7 460.7 all-reduce.2
where the time goes:
time: 829 us; the launch traced here: 828 us
  waiting for transfers between devices  482 us (58%)
  blocking collectives  276 us (33%)
  matrix products  30.4 us (4%)
  local copies, waits for them, and re-layouts  16.1 us (2%)
  between operations  14.9 us (2%)
  other arithmetic  9.12 us (1%)
    psum x1, waiting for transfers between devices, on_device(): left_all = lax.psum(left_term, ('dp', 'tp'))  461 us
    psum x1, blocking collectives, on_device(): factor_next = lax.psum(right_term, 'dp') / lax.axis_size('dp')  276 us
    all_gather x1, waiting for transfers between devices, on_device(): lax.all_gather(layer_input, 'tp', axis=0, tiled=True)  20.1 us
  transfers between devices with their start and end apart: 2, of which 2 were waited for; matrix products, arithmetic and copies ran while one was open for 3% of the time, Pallas kernels for 0%

commit v1 on v0

v1 whole, which is shorter than its diff:
```python
import math

import jax
import jax.numpy as jnp
from jax import lax
from jax.experimental import pallas as pl
from jax.experimental.pallas import tpu as pltpu
from jax.sharding import PartitionSpec as P

MESH = pl.DeviceIdType.MESH
F32, BF16 = jnp.float32, jnp.bfloat16
NT = (((1,), (1,)), ((), ()))

NX, NY, NZ, NC = 4, 4, 16, 2
GROUP = NY * NC
PLANE = NX * GROUP

HEAD_DIM = 128
HEADS = 3
SLOTS = 1024
WIDTH = 2560
RANK = 32
LANES = 128
HALF = 16
FEATURES = HEADS * HEAD_DIM
TILES = WIDTH // LANES
MAIN = NX * NY
BLOCK = 256
BLOCKS = SLOTS // BLOCK
MASKED = -1e30


def hops(step, size):
    return min(step, size - step)


PLANE_STEPS = sorted(
    [
        (dx, dy, dc)
        for dx in range(NX)
        for dy in range(NY)
        for dc in range(NC)
        if (dx, dy, dc) != (0, 0, 0)
    ],
    key=lambda s: -(hops(s[0], NX) * 2 + hops(s[1], NY) * 2 + s[2]),
)
GROUP_STEPS = [s for s in PLANE_STEPS if s[0] == 0]
ROW_STEPS = sorted(range(1, NX), key=lambda s: -hops(s, NX))
DEPTH_STEPS = sorted(range(1, NZ), key=lambda s: -hops(s, NZ))
HOLDERS = [(xh, (xh + 2 * ch) % NY, ch) for ch in range(NC) for xh in range(NX)]


def segment_starts(seg, count):
    rows = lax.broadcasted_iota(jnp.int32, seg.shape, 0)
    lanes = lax.broadcasted_iota(jnp.int32, seg.shape, 1)
    slot = rows * LANES + lanes
    wrapped = pltpu.roll(seg, 1, 1)
    before = jnp.where(lanes == 0, pltpu.roll(wrapped, 1, 0), wrapped)
    first = jnp.where((seg != before) & (slot > 0), slot, 0)
    step = 1
    while step < LANES:
        first = jnp.maximum(first, jnp.where(lanes >= step, pltpu.roll(first, step, 1), 0))
        step *= 2
    carry = jnp.broadcast_to(jnp.max(first, axis=1, keepdims=True), first.shape)
    step = 1
    while step < SLOTS // LANES:
        carry = jnp.maximum(carry, jnp.where(rows >= step, pltpu.roll(carry, step, 0), 0))
        step *= 2
    first = jnp.maximum(first, jnp.where(rows >= 1, pltpu.roll(carry, 1, 0), 0))
    return jnp.where(slot < count, first, 4 * SLOTS)


def split(value):
    high = value.astype(BF16)
    low = (value - high.astype(F32)).astype(BF16)
    return jnp.concatenate([high, low], axis=0)


def attend(head, starts, k_ref, q_ref, g_ref, w_ref, v_ref):
    lanes = slice(head * HEAD_DIM, (head + 1) * HEAD_DIM)
    rate = HEAD_DIM ** (-0.5) * math.log2(math.e)
    for b in range(BLOCKS):
        low, high = b * BLOCK, (b + 1) * BLOCK
        q = q_ref[low:high, lanes]
        start = starts[b]
        live = start < SLOTS
        key = lax.broadcasted_iota(jnp.int32, (BLOCK, BLOCK), 0) + low
        query = lax.broadcasted_iota(jnp.int32, (BLOCK, BLOCK), 1) + low
        near = lax.dot_general(k_ref[low:high, lanes], q, NT, preferred_element_type=F32)
        near = jnp.where((key >= start) & (key <= query), near, MASKED)
        top = jnp.max(near, axis=0, keepdims=True)
        if b:
            far = lax.dot_general(k_ref[0:low, lanes], q, NT, preferred_element_type=F32)
            far_key = lax.broadcasted_iota(jnp.int32, (low, BLOCK), 0)
            far = jnp.where(far_key >= start, far, MASKED)
            top = jnp.maximum(top, jnp.max(far, axis=0, keepdims=True))
        near = jnp.exp2((near - top) * rate)
        total = jnp.sum(near, axis=0, keepdims=True)
        if b:
            far = jnp.exp2((far - top) * rate)
            total = total + jnp.sum(far, axis=0, keepdims=True)
        scale = jnp.where(live, 1.0 / jnp.maximum(total, 1.0), 0.0)
        w_ref[low:high, low:high] = (near * scale).astype(BF16)
        if b:
            w_ref[0:low, low:high] = (far * scale).astype(BF16)
    for b in range(BLOCKS):
        low, high = b * BLOCK, (b + 1) * BLOCK
        v = jnp.dot(w_ref[low:high, low:], g_ref[low:, lanes], preferred_element_type=F32)
        v_ref[low:high, lanes] = v.astype(BF16)


def kernel(
    layer_ref, q_hbm, k_hbm, g_hbm, feedback_ref, factor_ref, count_ref, segment_ref,
    basis_ref, next_ref,
    q_ref, k_ref, g_ref, f_ref, l_ref, v_ref, w_ref, pf_ref,
    zs_ref, zr_ref, part_ref, main_ref, extra_ref, deep_ref, left_ref, t_ref, ys_ref, xr_ref, deep2_ref, yf_ref,
    load_sem,
    a_send, a_recv, rs_send, rs_main, rs_extra, d_send, d_recv, ag_send, ag_main, ag_extra,
    t_send, t_recv, x_send, x_recv, d2_send, d2_recv, xg_send, xg_recv,
):
    dp, tp = lax.axis_index("dp"), lax.axis_index("tp")
    x, z = dp // NZ, dp % NZ
    y, c = tp // NC, tp % NC
    place = x * GROUP + tp

    def plane_peer(step):
        dx, dy, dc = step
        px, py, pc = (x + dx) % NX, (y + dy) % NY, (c + dc) % NC
        return px, py, pc

    def device(px, py, pc, pz):
        return (px * NZ + pz, py * NC + pc)

    barrier = pltpu.get_barrier_semaphore()
    for step in DEPTH_STEPS:
        pl.semaphore_signal(barrier, inc=1, device_id=device(x, y, c, (z + step) % NZ), device_id_type=MESH)
    for step in PLANE_STEPS:
        pl.semaphore_signal(barrier, inc=1, device_id=device(*plane_peer(step), z), device_id_type=MESH)

    loads = []

    def load(source, target):
        copy = pltpu.make_async_copy(source, target, load_sem.at[len(loads)])
        copy.start()
        loads.append(copy)

    for head in range(HEADS):
        lanes = pl.ds(head * HEAD_DIM, HEAD_DIM)
        for source, target in ((k_hbm, k_ref), (q_hbm, q_ref), (g_hbm, g_ref)):
            load(source.at[:, lanes], target.at[:, lanes])
    load(feedback_ref, f_ref)
    load(layer_ref, l_ref)

    def send(source, target, send_sem, recv_sem, where):
        copy = pltpu.make_async_remote_copy(
            src_ref=source, dst_ref=target, send_sem=send_sem, recv_sem=recv_sem,
            device_id=where, device_id_type=MESH,
        )
        copy.start()
        return copy

    def arrived(target, recv_sem):
        pltpu.make_async_copy(target, target, recv_sem).wait()

    starts = segment_starts(segment_ref[...], count_ref[0])
    per = BLOCK // LANES
    starts = [
        jnp.concatenate([starts[b * per + i:b * per + i + 1] for i in range(per)], axis=1) for b in range(BLOCKS)
    ]
    for head in range(HEADS):
        for copy in loads[3 * head:3 * head + 3]:
            copy.wait()
        attend(head, starts, k_ref, q_ref, g_ref, w_ref.at[head], v_ref)

    factor = split(factor_ref[...])
    for t in range(GROUP):
        got = lax.dot_general(factor, v_ref[t * LANES:(t + 1) * LANES, :], NT, preferred_element_type=F32)
        zs_ref[t] = got[:RANK] + got[RANK:]
    pl.semaphore_wait(barrier, len(DEPTH_STEPS) + len(PLANE_STEPS))
    a_copies = []
    for i, step in enumerate(GROUP_STEPS):
        px, py, pc = plane_peer(step)
        peer = py * NC + pc
        a_copies.append(send(zs_ref.at[peer], zr_ref.at[tp], a_send.at[i], a_recv.at[tp], (dp, peer)))
    zr_ref[tp] = zs_ref[tp]

    loads[9].wait()
    for j in range(WIDTH // BLOCK):
        got = lax.dot_general(factor, f_ref[j * BLOCK:(j + 1) * BLOCK, :], NT, preferred_element_type=F32)
        pf_ref[:, j * BLOCK:(j + 1) * BLOCK] = got[:RANK] + got[RANK:]
    loads[10].wait()

    for step in GROUP_STEPS:
        px, py, pc = plane_peer(step)
        peer = py * NC + pc
        arrived(zr_ref.at[peer], a_recv.at[peer])
    mixed = split(jnp.sum(zr_ref[...], axis=0))
    for j in range(WIDTH // BLOCK):
        lanes = slice(j * BLOCK, (j + 1) * BLOCK)
        got = jnp.dot(mixed, l_ref[:, lanes], preferred_element_type=F32)
        part = (pf_ref[:, lanes] + got[:RANK] + got[RANK:]).astype(BF16)
        for i in range(per):
            for h in range(NC):
                part_ref[h, j * per + i] = part[h * HALF:(h + 1) * HALF, i * LANES:(i + 1) * LANES]

    holder = y == (x + 2 * c) % NY
    own = 4 * x + y
    rs_copies, rs_extras = [], []
    for i, step in enumerate(PLANE_STEPS):
        px, py, pc = plane_peer(step)
        rs_copies.append(
            send(part_ref.at[pc, NY * px + py], main_ref.at[place], rs_send.at[i], rs_main.at[place], device(px, py, pc, z))
        )
    for i, (xh, yh, ch) in enumerate(HOLDERS):
        other = place != xh * GROUP + yh * NC + ch

        @pl.when(other)
        def _():
            send(
                part_ref.at[ch, MAIN + xh], extra_ref.at[place],
                rs_send.at[len(PLANE_STEPS) + i], rs_extra.at[place], device(xh, yh, ch, z),
            )

    main_ref[place] = part_ref[c, own]
    extra_ref[place] = part_ref[c, MAIN + x]
    for copy in a_copies:
        copy.wait_send()
    for step in PLANE_STEPS:
        px, py, pc = plane_peer(step)
        peer = px * GROUP + py * NC + pc
        arrived(main_ref.at[peer], rs_main.at[peer])
    deep_ref[0, z] = jnp.sum(main_ref[...].astype(F32), axis=0).astype(BF16)
    d_copies = []
    for i, step in enumerate(DEPTH_STEPS):
        d_copies.append(
            send(deep_ref.at[0, z], deep_ref.at[0, z], d_send.at[0, i], d_recv.at[0, z], device(x, y, c, (z + step) % NZ))
        )

    @pl.when(holder)
    def _():
        for step in PLANE_STEPS:
            px, py, pc = plane_peer(step)
            peer = px * GROUP + py * NC + pc
            arrived(extra_ref.at[peer], rs_extra.at[peer])
        deep_ref[1, z] = jnp.sum(extra_ref[...].astype(F32), axis=0).astype(BF16)
        for i, step in enumerate(DEPTH_STEPS):
            send(deep_ref.at[1, z], deep_ref.at[1, z], d_send.at[1, i], d_recv.at[1, z], device(x, y, c, (z + step) % NZ))

    for copy in rs_copies:
        copy.wait_send()
    for i, (xh, yh, ch) in enumerate(HOLDERS):
        other = place != xh * GROUP + yh * NC + ch

        @pl.when(other)
        def _():
            arrived(part_ref.at[ch, MAIN + xh], rs_send.at[len(PLANE_STEPS) + i])

    for step in DEPTH_STEPS:
        peer = (z + step) % NZ
        arrived(deep_ref.at[0, peer], d_recv.at[0, peer])
    left_ref[c, own] = jnp.sum(deep_ref[0].astype(F32), axis=0).astype(BF16)
    ag_copies = []
    for i, step in enumerate(PLANE_STEPS):
        ag_copies.append(
            send(left_ref.at[c, own], left_ref.at[c, own], ag_send.at[0, i], ag_main.at[place], device(*plane_peer(step), z))
        )

    @pl.when(holder)
    def _():
        for step in DEPTH_STEPS:
            peer = (z + step) % NZ
            arrived(deep_ref.at[1, peer], d_recv.at[1, peer])
        left_ref[c, MAIN + x] = jnp.sum(deep_ref[1].astype(F32), axis=0).astype(BF16)
        for i, step in enumerate(PLANE_STEPS):
            send(
                left_ref.at[c, MAIN + x], left_ref.at[c, MAIN + x],
                ag_send.at[1, i], ag_extra.at[c * NX + x], device(*plane_peer(step), z),
            )

    for copy in d_copies:
        copy.wait_send()

    @pl.when(holder)
    def _():
        for i, step in enumerate(DEPTH_STEPS):
            arrived(deep_ref.at[1, z], d_send.at[1, i])

    for step in PLANE_STEPS:
        px, py, pc = plane_peer(step)
        arrived(left_ref.at[pc, NY * px + py], ag_main.at[px * GROUP + py * NC + pc])
    for i, (xh, yh, ch) in enumerate(HOLDERS):
        other = place != xh * GROUP + yh * NC + ch

        @pl.when(other)
        def _():
            arrived(left_ref.at[ch, MAIN + xh], ag_extra.at[i])

    left = jnp.concatenate(
        [jnp.concatenate([left_ref[h, n] for h in range(NC)], axis=0) for n in range(TILES)], axis=1
    )
    t_ref[tp] = lax.dot_general(left, l_ref[...], NT, preferred_element_type=F32).astype(BF16)
    t_copies = []
    for i, step in enumerate(GROUP_STEPS):
        px, py, pc = plane_peer(step)
        t_copies.append(send(t_ref.at[tp], t_ref.at[tp], t_send.at[i], t_recv.at[tp], (dp, py * NC + pc)))
    right = jnp.dot(left, f_ref[...], preferred_element_type=F32)
    for copy in ag_copies:
        copy.wait_send()

    @pl.when(holder)
    def _():
        for i, step in enumerate(PLANE_STEPS):
            arrived(left_ref.at[c, MAIN + x], ag_send.at[1, i])

    for step in GROUP_STEPS:
        px, py, pc = plane_peer(step)
        peer = py * NC + pc
        arrived(t_ref.at[peer], t_recv.at[peer])
    gathered = jnp.concatenate([t_ref[t] for t in range(GROUP)], axis=1)
    right = right + jnp.dot(gathered, v_ref[...], preferred_element_type=F32)

    for j in range(FEATURES // LANES):
        for h in range(NC):
            ys_ref[j * NC + h] = right[h * HALF:(h + 1) * HALF, j * LANES:(j + 1) * LANES]
    keeper = x // 2 == c
    spare = NX + x % 2
    x_copies = []
    for i, step in enumerate(ROW_STEPS):
        px = (x + step) % NX
        x_copies.append(send(ys_ref.at[px], xr_ref.at[0, x], x_send.at[i], x_recv.at[0, x], device(px, y, c, z)))
    for e in range(2):
        px = 2 * c + e

        @pl.when(x != px)
        def _():
            send(ys_ref.at[NX + e], xr_ref.at[1, x], x_send.at[NX - 1 + e], x_recv.at[1, x], device(px, y, c, z))

    xr_ref[0, x] = ys_ref[x]
    xr_ref[1, x] = ys_ref[spare]
    for copy in t_copies:
        copy.wait_send()
    for step in ROW_STEPS:
        px = (x + step) % NX
        arrived(xr_ref.at[0, px], x_recv.at[0, px])
    deep2_ref[0, z] = jnp.sum(xr_ref[0], axis=0).astype(BF16)
    d2_copies = []
    for i, step in enumerate(DEPTH_STEPS):
        d2_copies.append(
            send(deep2_ref.at[0, z], deep2_ref.at[0, z], d2_send.at[0, i], d2_recv.at[0, z], device(x, y, c, (z + step) % NZ))
        )

    @pl.when(keeper)
    def _():
        for step in ROW_STEPS:
            px = (x + step) % NX
            arrived(xr_ref.at[1, px], x_recv.at[1, px])
        deep2_ref[1, z] = jnp.sum(xr_ref[1], axis=0).astype(BF16)
        for i, step in enumerate(DEPTH_STEPS):
            send(deep2_ref.at[1, z], deep2_ref.at[1, z], d2_send.at[1, i], d2_recv.at[1, z], device(x, y, c, (z + step) % NZ))

    for copy in x_copies:
        copy.wait_send()
    for e in range(2):

        @pl.when(x != 2 * c + e)
        def _():
            arrived(ys_ref.at[NX + e], x_send.at[NX - 1 + e])

    tall = jnp.concatenate([left, jnp.zeros((LANES - RANK, WIDTH), BF16)], axis=0)
    table = lax.dot_general(left, tall, NT, preferred_element_type=F32)
    rows = lax.broadcasted_iota(jnp.int32, (RANK, LANES), 0)
    lanes = lax.broadcasted_iota(jnp.int32, (RANK, LANES), 1)
    table = jnp.where(lanes == rows + RANK, 1.0, table)
    for k in range(RANK):
        ratio = table[:, k:k + 1] / table[k:k + 1, k:k + 1]
        table = table - jnp.where(rows > k, ratio, 0.0) * table[k:k + 1, :]
    pivots = jnp.sum(jnp.where(lanes == rows, table, 0.0), axis=1, keepdims=True)
    inverse = jnp.where(lanes >= RANK, table, 0.0) * lax.rsqrt(pivots)

    def solve(value):
        padded = jnp.concatenate(
            [jnp.zeros((RANK, FEATURES), F32), value, jnp.zeros((LANES - 2 * RANK, FEATURES), F32)], axis=0
        )
        return jnp.dot(inverse, padded, precision=lax.Precision.HIGHEST, preferred_element_type=F32)

    first = (5 * tp) // 2
    window = jnp.concatenate(
        [
            jnp.concatenate([left_ref[h, first + i] for h in range(NC)], axis=0).astype(F32)
            for i in range(FEATURES // LANES)
        ],
        axis=1,
    )
    own_basis = solve(window) * math.sqrt(WIDTH)
    shifted = jnp.concatenate(
        [own_basis[:, LANES // 2:], own_basis[:, :LANES // 2]], axis=1
    )
    share = WIDTH // GROUP
    basis_ref[...] = jnp.where(tp % 2 == 1, shifted, own_basis)[:, :share]

    for step in DEPTH_STEPS:
        peer = (z + step) % NZ
        arrived(deep2_ref.at[0, peer], d2_recv.at[0, peer])
    yf_ref[x] = jnp.sum(deep2_ref[0].astype(F32), axis=0)
    xg_copies = []
    for i, step in enumerate(ROW_STEPS):
        xg_copies.append(send(yf_ref.at[x], yf_ref.at[x], xg_send.at[0, i], xg_recv.at[x], device((x + step) % NX, y, c, z)))

    @pl.when(keeper)
    def _():
        for step in DEPTH_STEPS:
            peer = (z + step) % NZ
            arrived(deep2_ref.at[1, peer], d2_recv.at[1, peer])
        yf_ref[spare] = jnp.sum(deep2_ref[1].astype(F32), axis=0)
        for i, step in enumerate(ROW_STEPS):
            send(yf_ref.at[spare], yf_ref.at[spare], xg_send.at[1, i], xg_recv.at[spare], device((x + step) % NX, y, c, z))

    for copy in d2_copies:
        copy.wait_send()

    @pl.when(keeper)
    def _():
        for i, step in enumerate(DEPTH_STEPS):
            arrived(deep2_ref.at[1, z], d2_send.at[1, i])

    for step in ROW_STEPS:
        px = (x + step) % NX
        arrived(yf_ref.at[px], xg_recv.at[px])
    for e in range(2):

        @pl.when(x != 2 * c + e)
        def _():
            arrived(yf_ref.at[NX + e], xg_recv.at[NX + e])

    summed = jnp.concatenate(
        [
            jnp.concatenate([yf_ref[j * NC + h] for h in range(NC)], axis=0)
            for j in range(FEATURES // LANES)
        ],
        axis=1,
    )
    next_ref[...] = solve(summed) * (1.0 / (NX * NZ))
    for copy in xg_copies:
        copy.wait_send()

    @pl.when(keeper)
    def _():
        for i, step in enumerate(ROW_STEPS):
            arrived(yf_ref.at[spare], xg_send.at[1, i])


def on_device(
    layer_input, queries, key_vectors, out_grad, feedback, factor_prev, token_count, segment_ids
):
    vmem = pl.BlockSpec(memory_space=pltpu.VMEM)
    anywhere = pl.BlockSpec(memory_space=pl.ANY)
    dma = pltpu.SemaphoreType.DMA
    plane = PLANE - 1
    deep = NZ - 1
    return pl.pallas_call(
        kernel,
        out_shape=(
            jax.ShapeDtypeStruct((RANK, WIDTH // GROUP), F32),
            jax.ShapeDtypeStruct((RANK, FEATURES), F32),
        ),
        in_specs=[anywhere] * 5 + [vmem, pl.BlockSpec(memory_space=pltpu.SMEM), vmem],
        out_specs=(vmem, vmem),
        scratch_shapes=[
            pltpu.VMEM((SLOTS, FEATURES), BF16),
            pltpu.VMEM((SLOTS, FEATURES), BF16),
            pltpu.VMEM((SLOTS, FEATURES), BF16),
            pltpu.VMEM((WIDTH, FEATURES), BF16),
            pltpu.VMEM((LANES, WIDTH), BF16),
            pltpu.VMEM((SLOTS, FEATURES), BF16),
            pltpu.VMEM((HEADS, SLOTS, SLOTS), BF16),
            pltpu.VMEM((RANK, WIDTH), F32),
            pltpu.VMEM((GROUP, RANK, LANES), F32),
            pltpu.VMEM((GROUP, RANK, LANES), F32),
            pltpu.VMEM((NC, TILES, HALF, LANES), BF16),
            pltpu.VMEM((PLANE, HALF, LANES), BF16),
            pltpu.VMEM((PLANE, HALF, LANES), BF16),
            pltpu.VMEM((2, NZ, HALF, LANES), BF16),
            pltpu.VMEM((NC, TILES, HALF, LANES), BF16),
            pltpu.VMEM((GROUP, RANK, LANES), BF16),
            pltpu.VMEM((6, HALF, LANES), F32),
            pltpu.VMEM((2, NX, HALF, LANES), F32),
            pltpu.VMEM((2, NZ, HALF, LANES), BF16),
            pltpu.VMEM((6, HALF, LANES), F32),
            dma((11,)),
            dma((GROUP - 1,)), dma((GROUP,)),
            dma((plane + len(HOLDERS),)), dma((PLANE,)), dma((PLANE,)),
            dma((2, deep)), dma((2, NZ)),
            dma((2, plane)), dma((PLANE,)), dma((len(HOLDERS),)),
            dma((GROUP - 1,)), dma((GROUP,)),
            dma((NX + 1,)), dma((2, NX)),
            dma((2, deep)), dma((2, NZ)),
            dma((2, NX - 1)), dma((6,)),
        ],
        compiler_params=pltpu.CompilerParams(
            collective_id=0, has_side_effects=True, vmem_limit_bytes=60 * 1024 * 1024
        ),
    )(
        layer_input, queries, key_vectors, out_grad, feedback, factor_prev, token_count,
        segment_ids.reshape(SLOTS // LANES, LANES),
    )


def solution(mesh):
    return jax.shard_map(
        on_device,
        mesh=mesh,
        in_specs=(
            P(("dp", "tp"), None),
            P("dp", "tp"),
            P("dp", "tp"),
            P("dp", "tp"),
            P("dp", "tp"),
            P(None, "tp"),
            P("dp"),
            P("dp"),
        ),
        out_specs=(P(None, "tp"), P(None, "tp")),
        check_vma=False,
    )
```

time: 829 us -> 67.4 us (0.08)
  the two profiles are of different devices: /device:TPU:8 before, /device:TPU:6 now
where the time goes in v1:
time: 67.4 us; the launch traced here: 66.5 us
  Pallas kernels  62.4 us (93%)
  local copies, waits for them, and re-layouts  2.84 us (4%)
  between operations  1.29 us (2%)
    pallas_call x1, Pallas kernels, on_device(): pl.pallas_call(kernel, out_shape=(jax.ShapeDtypeStruct((RANK, WIDTH // GR...  62.4 us
    unnamed x2, local copies, waits for them, and re-layouts  2.84 us

profile of v1, /device:TPU:6, one launch (start us, length us, event | category | flops | bytes accessed | tf_op | source)
XLA Modules:
  0.0 66.5 jit_solution(2728424310534138063)
XLA Ops:
  1.3 62.4 %shard_map.95 = (f32[32,320]{1,0:T(8,128)}, f32[32,384]{1,0:T(8,128)}) custom-call(bf16[128,2560]{1,0:T(8,128)(2,1)} %layer_ref.1, bf16[1024,384]{1,0:T(8,128)(2,1)} %q_hbm.1, bf16[1024,384]{1,0:T(8,128)(2,1)} %k_hbm.1, bf16[1024,384]{1,0:T(8,128)(2,1)} %g_hbm.1, bf16[2560,384]{1,0:T(8,128)(2,1)} %feedback_ref.1, f32[32,384]{1,0:T(8,128)} %factor_ref.1, ...), custom_call_target="tpu_custom_call" | custom-call | tf_op jit(solution)/shard_map/pallas_call | solution.py:460
  63.7 1.4 %copy.13 = f32[32,320]{1,0:T(8,128)} copy(f32[32,320]{1,0:T(8,128)} %get-tuple-element.4) | data formatting | bytes 81920
  65.1 1.4 %copy.14 = f32[32,384]{1,0:T(8,128)} copy(f32[32,384]{1,0:T(8,128)} %get-tuple-element.5) | data formatting | bytes 98304

commit v2 on v1

v2 whole, which is shorter than its diff:
```python
import math

import jax
import jax.numpy as jnp
from jax import lax
from jax.experimental import pallas as pl
from jax.experimental.pallas import tpu as pltpu
from jax.sharding import PartitionSpec as P

MESH = pl.DeviceIdType.MESH
F32, BF16 = jnp.float32, jnp.bfloat16
NT = (((1,), (1,)), ((), ()))

NX, NY, NZ, NC = 4, 4, 16, 2
GROUP = NY * NC
PLANE = NX * GROUP
OTHERS = PLANE - 1
DEEP = NZ - 1

HEAD_DIM = 128
HEADS = 3
SLOTS = 1024
WIDTH = 2560
RANK = 32
LANES = 128
HALF = 16
FEATURES = HEADS * HEAD_DIM
TILES = WIDTH // LANES
MAIN = NX * NY
BLOCK = 256
BLOCKS = SLOTS // BLOCK
MASKED = -1e30


def ahead(position, step, size):
    moved = position + step
    return jnp.where(moved >= size, moved - size, moved) if step else position


def hops(step, size):
    return min(step, size - step)


PLANE_STEPS = sorted(
    [
        (dx, dy, dc)
        for dx in range(NX)
        for dy in range(NY)
        for dc in range(NC)
        if (dx, dy, dc) != (0, 0, 0)
    ],
    key=lambda s: -(hops(s[0], NX) * 2 + hops(s[1], NY) * 2 + s[2]),
)
GROUP_STEPS = [s for s in PLANE_STEPS if s[0] == 0]
ROW_STEPS = sorted(range(1, NX), key=lambda s: -hops(s, NX))
DEPTH_STEPS = sorted(range(1, NZ), key=lambda s: -hops(s, NZ))
HOLDERS = [(xh, (xh + 2 * ch) % NY, ch) for ch in range(NC) for xh in range(NX)]


def segment_starts(seg, count):
    rows = lax.broadcasted_iota(jnp.int32, seg.shape, 0)
    lanes = lax.broadcasted_iota(jnp.int32, seg.shape, 1)
    slot = rows * LANES + lanes
    wrapped = pltpu.roll(seg, 1, 1)
    before = jnp.where(lanes == 0, pltpu.roll(wrapped, 1, 0), wrapped)
    first = jnp.where((seg != before) & (slot > 0), slot, 0)
    step = 1
    while step < LANES:
        first = jnp.maximum(first, jnp.where(lanes >= step, pltpu.roll(first, step, 1), 0))
        step *= 2
    carry = jnp.broadcast_to(jnp.max(first, axis=1, keepdims=True), first.shape)
    step = 1
    while step < SLOTS // LANES:
        carry = jnp.maximum(carry, jnp.where(rows >= step, pltpu.roll(carry, step, 0), 0))
        step *= 2
    first = jnp.maximum(first, jnp.where(rows >= 1, pltpu.roll(carry, 1, 0), 0))
    return jnp.where(slot < count, first, 4 * SLOTS)


def split(value):
    high = value.astype(BF16)
    low = (value - high.astype(F32)).astype(BF16)
    return jnp.concatenate([high, low], axis=0)


def attend(head, starts, k_ref, q_ref, g_ref, w_ref, v_ref):
    lanes = slice(head * HEAD_DIM, (head + 1) * HEAD_DIM)
    rate = HEAD_DIM ** (-0.5) * math.log2(math.e)
    for b in range(BLOCKS):
        low, high = b * BLOCK, (b + 1) * BLOCK
        q = q_ref[low:high, lanes]
        start = starts[b]
        live = start < SLOTS
        key = lax.broadcasted_iota(jnp.int32, (BLOCK, BLOCK), 0) + low
        query = lax.broadcasted_iota(jnp.int32, (BLOCK, BLOCK), 1) + low
        near = lax.dot_general(k_ref[low:high, lanes], q, NT, preferred_element_type=F32)
        near = jnp.where((key >= start) & (key <= query), near, MASKED)
        top = jnp.max(near, axis=0, keepdims=True)
        if b:
            far = lax.dot_general(k_ref[0:low, lanes], q, NT, preferred_element_type=F32)
            far_key = lax.broadcasted_iota(jnp.int32, (low, BLOCK), 0)
            far = jnp.where(far_key >= start, far, MASKED)
            top = jnp.maximum(top, jnp.max(far, axis=0, keepdims=True))
        near = jnp.exp2((near - top) * rate)
        total = jnp.sum(near, axis=0, keepdims=True)
        if b:
            far = jnp.exp2((far - top) * rate)
            total = total + jnp.sum(far, axis=0, keepdims=True)
        scale = jnp.where(live, 1.0 / jnp.maximum(total, 1.0), 0.0)
        w_ref[low:high, low:high] = (near * scale).astype(BF16)
        if b:
            w_ref[0:low, low:high] = (far * scale).astype(BF16)
    for b in range(BLOCKS):
        low, high = b * BLOCK, (b + 1) * BLOCK
        v = jnp.dot(w_ref[low:high, low:], g_ref[low:, lanes], preferred_element_type=F32)
        v_ref[low:high, lanes] = v.astype(BF16)


def kernel(
    layer_hbm, q_hbm, k_hbm, g_hbm, feedback_hbm, factor_hbm, count_ref, segment_hbm,
    basis_ref, next_ref,
    factor_ref, segment_ref,
    q_ref, k_ref, g_ref, f_ref, l_ref, v_ref, w_ref, pf_ref,
    zs_ref, zr_ref, part_ref, main_ref, extra_ref, deep_ref, left_ref, t_ref, ys_ref, xr_ref, deep2_ref, yf_ref,
    load_sem,
    a_send, a_recv, rs_send, rs_recv, d_send, d_recv, ag_send, ag_recv,
    t_send, t_recv, x_send, x_recv, d2_send, d2_recv, xg_send, xg_recv,
):
    dp, tp = lax.axis_index("dp"), lax.axis_index("tp")
    x, z = dp // NZ, dp % NZ
    y, c = tp // NC, tp % NC
    place = x * GROUP + tp

    def plane_peer(step):
        dx, dy, dc = step
        return ahead(x, dx, NX), ahead(y, dy, NY), 1 - c if dc else c

    def device(px, py, pc, pz):
        return (px * NZ + pz, py * NC + pc)

    def load(source, target, which):
        pltpu.make_async_copy(source, target, load_sem.at[which]).start()

    def load_head(head):
        lanes = pl.ds(head * HEAD_DIM, HEAD_DIM)
        for source, target in ((k_hbm, k_ref), (q_hbm, q_ref), (g_hbm, g_ref)):
            load(source.at[:, lanes], target.at[:, lanes], head)

    load(segment_hbm, segment_ref, HEADS)
    load_head(0)
    barrier = pltpu.get_barrier_semaphore()
    for step in DEPTH_STEPS:
        pl.semaphore_signal(barrier, inc=1, device_id=device(x, y, c, ahead(z, step, NZ)), device_id_type=MESH)
    for step in PLANE_STEPS:
        pl.semaphore_signal(barrier, inc=1, device_id=device(*plane_peer(step), z), device_id_type=MESH)
    for head in range(1, HEADS):
        load_head(head)
    load(factor_hbm, factor_ref, HEADS + 1)
    load(feedback_hbm, f_ref, HEADS + 2)
    load(layer_hbm, l_ref, HEADS + 3)

    def send(source, target, send_sem, recv_sem, where):
        pltpu.make_async_remote_copy(
            src_ref=source, dst_ref=target, send_sem=send_sem, recv_sem=recv_sem,
            device_id=where, device_id_type=MESH,
        ).start()

    def arrived(target, recv_sem):
        pltpu.make_async_copy(target, target, recv_sem).wait()

    arrived(segment_ref, load_sem.at[HEADS])
    starts = segment_starts(segment_ref[...], count_ref[0])
    per = BLOCK // LANES
    starts = [
        jnp.concatenate([starts[b * per + i:b * per + i + 1] for i in range(per)], axis=1) for b in range(BLOCKS)
    ]
    for head in range(HEADS):
        arrived(k_ref, load_sem.at[head])
        attend(head, starts, k_ref, q_ref, g_ref, w_ref.at[head], v_ref)

    arrived(factor_ref, load_sem.at[HEADS + 1])
    factor = split(factor_ref[...])
    for t in range(GROUP):
        got = lax.dot_general(factor, v_ref[t * LANES:(t + 1) * LANES, :], NT, preferred_element_type=F32)
        zs_ref[t] = got[:RANK] + got[RANK:]
    pl.semaphore_wait(barrier, len(DEPTH_STEPS) + len(PLANE_STEPS))
    for step in GROUP_STEPS:
        px, py, pc = plane_peer(step)
        peer = py * NC + pc
        send(zs_ref.at[peer], zr_ref.at[tp], a_send, a_recv, (dp, peer))
    zr_ref[tp] = zs_ref[tp]

    arrived(f_ref, load_sem.at[HEADS + 2])
    for j in range(WIDTH // BLOCK):
        got = lax.dot_general(factor, f_ref[j * BLOCK:(j + 1) * BLOCK, :], NT, preferred_element_type=F32)
        pf_ref[:, j * BLOCK:(j + 1) * BLOCK] = got[:RANK] + got[RANK:]
    arrived(l_ref, load_sem.at[HEADS + 3])
    arrived(zs_ref.at[pl.ds(0, GROUP - 1)], a_send)
    arrived(zr_ref.at[pl.ds(0, GROUP - 1)], a_recv)
    mixed = split(jnp.sum(zr_ref[...], axis=0))
    for j in range(WIDTH // BLOCK):
        lanes = slice(j * BLOCK, (j + 1) * BLOCK)
        got = jnp.dot(mixed, l_ref[:, lanes], preferred_element_type=F32)
        part = (pf_ref[:, lanes] + got[:RANK] + got[RANK:]).astype(BF16)
        for i in range(per):
            for h in range(NC):
                part_ref[h * TILES + j * per + i] = part[h * HALF:(h + 1) * HALF, i * LANES:(i + 1) * LANES]

    holder = y == (x + 2 * c) % NY
    own = c * TILES + NY * x + y
    spare = c * TILES + MAIN + x
    for step in PLANE_STEPS:
        px, py, pc = plane_peer(step)
        send(part_ref.at[pc * TILES + NY * px + py], main_ref.at[place], rs_send.at[0], rs_recv.at[0], device(px, py, pc, z))
    for xh, yh, ch in HOLDERS:

        @pl.when(place != xh * GROUP + yh * NC + ch)
        def _():
            send(part_ref.at[ch * TILES + MAIN + xh], extra_ref.at[place], rs_send.at[1], rs_recv.at[1], device(xh, yh, ch, z))

    main_ref[place] = part_ref[own]
    extra_ref[place] = part_ref[spare]
    arrived(main_ref.at[pl.ds(0, OTHERS)], rs_recv.at[0])
    deep_ref[0, z] = jnp.sum(main_ref[...].astype(F32), axis=0).astype(BF16)

    def drain_scatter():
        arrived(part_ref.at[pl.ds(0, OTHERS)], rs_send.at[0])

        @pl.when(holder)
        def _():
            arrived(part_ref.at[pl.ds(0, len(HOLDERS) - 1)], rs_send.at[1])

        @pl.when(jnp.logical_not(holder))
        def _():
            arrived(part_ref.at[pl.ds(0, len(HOLDERS))], rs_send.at[1])

    deep_device = [device(x, y, c, ahead(z, step, NZ)) for step in DEPTH_STEPS]
    for where in deep_device:
        send(deep_ref.at[0, z], deep_ref.at[0, z], d_send.at[0], d_recv.at[0], where)

    @pl.when(holder)
    def _():
        arrived(extra_ref.at[pl.ds(0, OTHERS)], rs_recv.at[1])
        deep_ref[1, z] = jnp.sum(extra_ref[...].astype(F32), axis=0).astype(BF16)
        for where in deep_device:
            send(deep_ref.at[1, z], deep_ref.at[1, z], d_send.at[1], d_recv.at[1], where)

    drain_scatter()
    arrived(deep_ref.at[0, pl.ds(0, DEEP)], d_recv.at[0])
    left_ref[own] = jnp.sum(deep_ref[0].astype(F32), axis=0).astype(BF16)

    def drain_depth():
        arrived(deep_ref.at[0, pl.ds(0, DEEP)], d_send.at[0])

        @pl.when(holder)
        def _():
            arrived(deep_ref.at[1, pl.ds(0, DEEP)], d_send.at[1])

    plane_device = [device(*plane_peer(step), z) for step in PLANE_STEPS]
    for where in plane_device:
        send(left_ref.at[own], left_ref.at[own], ag_send.at[0], ag_recv.at[0], where)

    @pl.when(holder)
    def _():
        arrived(deep_ref.at[1, pl.ds(0, DEEP)], d_recv.at[1])
        left_ref[spare] = jnp.sum(deep_ref[1].astype(F32), axis=0).astype(BF16)
        for where in plane_device:
            send(left_ref.at[spare], left_ref.at[spare], ag_send.at[1], ag_recv.at[1], where)

    drain_depth()
    arrived(left_ref.at[pl.ds(0, OTHERS)], ag_recv.at[0])

    @pl.when(holder)
    def _():
        arrived(left_ref.at[pl.ds(0, len(HOLDERS) - 1)], ag_recv.at[1])

    @pl.when(jnp.logical_not(holder))
    def _():
        arrived(left_ref.at[pl.ds(0, len(HOLDERS))], ag_recv.at[1])

    def drain_gather():
        arrived(left_ref.at[pl.ds(0, OTHERS)], ag_send.at[0])

        @pl.when(holder)
        def _():
            arrived(left_ref.at[pl.ds(0, OTHERS)], ag_send.at[1])


    left = jnp.concatenate(
        [jnp.concatenate([left_ref[h * TILES + n] for h in range(NC)], axis=0) for n in range(TILES)], axis=1
    )
    t_ref[tp] = lax.dot_general(left, l_ref[...], NT, preferred_element_type=F32).astype(BF16)
    for step in GROUP_STEPS:
        px, py, pc = plane_peer(step)
        send(t_ref.at[tp], t_ref.at[tp], t_send, t_recv, (dp, py * NC + pc))
    right = jnp.dot(left, f_ref[...], preferred_element_type=F32)
    drain_gather()
    arrived(t_ref.at[pl.ds(0, GROUP - 1)], t_recv)
    gathered = jnp.concatenate([t_ref[t] for t in range(GROUP)], axis=1)
    right = right + jnp.dot(gathered, v_ref[...], preferred_element_type=F32)

    for j in range(FEATURES // LANES):
        for h in range(NC):
            ys_ref[j * NC + h] = right[h * HALF:(h + 1) * HALF, j * LANES:(j + 1) * LANES]
    keeper = x // 2 == c
    odd = NX + x % 2
    row_device = [device(ahead(x, step, NX), y, c, z) for step in ROW_STEPS]
    for step, where in zip(ROW_STEPS, row_device):
        send(ys_ref.at[ahead(x, step, NX)], xr_ref.at[0, x], x_send.at[0], x_recv.at[0], where)
    for e in range(2):

        @pl.when(x != 2 * c + e)
        def _():
            send(ys_ref.at[NX + e], xr_ref.at[1, x], x_send.at[1 + e], x_recv.at[1], device(2 * c + e, y, c, z))

    xr_ref[0, x] = ys_ref[x]
    xr_ref[1, x] = ys_ref[odd]
    arrived(xr_ref.at[0, pl.ds(0, NX - 1)], x_recv.at[0])
    deep2_ref[0, z] = jnp.sum(xr_ref[0], axis=0).astype(BF16)

    def drain_rows():
        arrived(t_ref.at[pl.ds(0, GROUP - 1)], t_send)
        arrived(ys_ref.at[pl.ds(0, NX - 1)], x_send.at[0])
        for e in range(2):

            @pl.when(x != 2 * c + e)
            def _():
                arrived(ys_ref.at[NX + e], x_send.at[1 + e])

    for where in deep_device:
        send(deep2_ref.at[0, z], deep2_ref.at[0, z], d2_send.at[0], d2_recv.at[0], where)

    @pl.when(keeper)
    def _():
        arrived(xr_ref.at[1, pl.ds(0, NX - 1)], x_recv.at[1])
        deep2_ref[1, z] = jnp.sum(xr_ref[1], axis=0).astype(BF16)
        for where in deep_device:
            send(deep2_ref.at[1, z], deep2_ref.at[1, z], d2_send.at[1], d2_recv.at[1], where)

    drain_rows()

    tall = jnp.concatenate([left, jnp.zeros((LANES - RANK, WIDTH), BF16)], axis=0)
    table = lax.dot_general(left, tall, NT, preferred_element_type=F32)
    rows = lax.broadcasted_iota(jnp.int32, (RANK, LANES), 0)
    lanes = lax.broadcasted_iota(jnp.int32, (RANK, LANES), 1)
    table = jnp.where(lanes == rows + RANK, 1.0, table)
    for k in range(RANK):
        ratio = table[:, k:k + 1] / table[k:k + 1, k:k + 1]
        table = table - jnp.where(rows > k, ratio, 0.0) * table[k:k + 1, :]
    pivots = jnp.sum(jnp.where(lanes == rows, table, 0.0), axis=1, keepdims=True)
    inverse = jnp.where(lanes >= RANK, table, 0.0) * lax.rsqrt(pivots)

    def solve(value):
        padded = jnp.concatenate(
            [jnp.zeros((RANK, FEATURES), F32), value, jnp.zeros((LANES - 2 * RANK, FEATURES), F32)], axis=0
        )
        return jnp.dot(inverse, padded, precision=lax.Precision.HIGHEST, preferred_element_type=F32)

    first = (5 * tp) // 2
    window = jnp.concatenate(
        [
            jnp.concatenate([left_ref[h * TILES + first + i] for h in range(NC)], axis=0).astype(F32)
            for i in range(FEATURES // LANES)
        ],
        axis=1,
    )
    own_basis = solve(window) * math.sqrt(WIDTH)
    shifted = jnp.concatenate([own_basis[:, LANES // 2:], own_basis[:, :LANES // 2]], axis=1)
    share = WIDTH // GROUP
    basis_ref[...] = jnp.where(tp % 2 == 1, shifted, own_basis)[:, :share]

    def drain_depth2():
        arrived(deep2_ref.at[0, pl.ds(0, DEEP)], d2_send.at[0])

        @pl.when(keeper)
        def _():
            arrived(deep2_ref.at[1, pl.ds(0, DEEP)], d2_send.at[1])

    arrived(deep2_ref.at[0, pl.ds(0, DEEP)], d2_recv.at[0])
    yf_ref[x] = jnp.sum(deep2_ref[0].astype(F32), axis=0)
    for where in row_device:
        send(yf_ref.at[x], yf_ref.at[x], xg_send.at[0], xg_recv.at[0], where)

    @pl.when(keeper)
    def _():
        arrived(deep2_ref.at[1, pl.ds(0, DEEP)], d2_recv.at[1])
        yf_ref[odd] = jnp.sum(deep2_ref[1].astype(F32), axis=0)
        for where in row_device:
            send(yf_ref.at[odd], yf_ref.at[odd], xg_send.at[1], xg_recv.at[1 + x % 2], where)

    drain_depth2()
    arrived(yf_ref.at[pl.ds(0, NX - 1)], xg_recv.at[0])
    for e in range(2):

        @pl.when(x != 2 * c + e)
        def _():
            arrived(yf_ref.at[NX + e], xg_recv.at[1 + e])

    summed = jnp.concatenate(
        [
            jnp.concatenate([yf_ref[j * NC + h] for h in range(NC)], axis=0)
            for j in range(FEATURES // LANES)
        ],
        axis=1,
    )
    next_ref[...] = solve(summed) * (1.0 / (NX * NZ))
    arrived(yf_ref.at[pl.ds(0, NX - 1)], xg_send.at[0])

    @pl.when(keeper)
    def _():
        arrived(yf_ref.at[pl.ds(0, NX - 1)], xg_send.at[1])


def on_device(
    layer_input, queries, key_vectors, out_grad, feedback, factor_prev, token_count, segment_ids
):
    vmem = pl.BlockSpec(memory_space=pltpu.VMEM)
    anywhere = pl.BlockSpec(memory_space=pltpu.HBM)
    dma = pltpu.SemaphoreType.DMA
    return pl.pallas_call(
        kernel,
        out_shape=(
            jax.ShapeDtypeStruct((RANK, WIDTH // GROUP), F32),
            jax.ShapeDtypeStruct((RANK, FEATURES), F32),
        ),
        in_specs=[anywhere] * 6 + [pl.BlockSpec(memory_space=pltpu.SMEM), anywhere],
        out_specs=(vmem, vmem),
        scratch_shapes=[
            pltpu.VMEM((RANK, FEATURES), F32),
            pltpu.VMEM((SLOTS // LANES, LANES), jnp.int32),
            pltpu.VMEM((SLOTS, FEATURES), BF16),
            pltpu.VMEM((SLOTS, FEATURES), BF16),
            pltpu.VMEM((SLOTS, FEATURES), BF16),
            pltpu.VMEM((WIDTH, FEATURES), BF16),
            pltpu.VMEM((LANES, WIDTH), BF16),
            pltpu.VMEM((SLOTS, FEATURES), BF16),
            pltpu.VMEM((HEADS, SLOTS, SLOTS), BF16),
            pltpu.VMEM((RANK, WIDTH), F32),
            pltpu.VMEM((GROUP, RANK, LANES), F32),
            pltpu.VMEM((GROUP, RANK, LANES), F32),
            pltpu.VMEM((NC * TILES, HALF, LANES), BF16),
            pltpu.VMEM((PLANE, HALF, LANES), BF16),
            pltpu.VMEM((PLANE, HALF, LANES), BF16),
            pltpu.VMEM((2, NZ, HALF, LANES), BF16),
            pltpu.VMEM((NC * TILES, HALF, LANES), BF16),
            pltpu.VMEM((GROUP, RANK, LANES), BF16),
            pltpu.VMEM((6, HALF, LANES), F32),
            pltpu.VMEM((2, NX, HALF, LANES), F32),
            pltpu.VMEM((2, NZ, HALF, LANES), BF16),
            pltpu.VMEM((6, HALF, LANES), F32),
            dma((HEADS + 4,)),
            dma, dma,
            dma((2,)), dma((2,)),
            dma((2,)), dma((2,)),
            dma((2,)), dma((2,)),
            dma, dma,
            dma((3,)), dma((2,)),
            dma((2,)), dma((2,)),
            dma((2,)), dma((3,)),
        ],
        compiler_params=pltpu.CompilerParams(
            collective_id=0, has_side_effects=True, vmem_limit_bytes=32 * 1024 * 1024
        ),
    )(
        *(
            pltpu.with_memory_space_constraint(value, pltpu.HBM)
            for value in (layer_input, queries, key_vectors, out_grad, feedback, factor_prev)
        ),
        token_count,
        pltpu.with_memory_space_constraint(segment_ids.reshape(SLOTS // LANES, LANES), pltpu.HBM),
    )


def solution(mesh):
    return jax.shard_map(
        on_device,
        mesh=mesh,
        in_specs=(
            P(("dp", "tp"), None),
            P("dp", "tp"),
            P("dp", "tp"),
            P("dp", "tp"),
            P("dp", "tp"),
            P(None, "tp"),
            P("dp"),
            P("dp"),
        ),
        out_specs=(P(None, "tp"), P(None, "tp")),
        check_vma=False,
    )
```

time: 67.4 us -> 60.4 us (0.90)
  Pallas kernels: 62.4 us -> 57.7 us
  local copies, waits for them, and re-layouts: 2.84 us -> 1.24 us
    pallas_call x1, Pallas kernels: 62.4 us -> 57.7 us  [on_device(): pl.pallas_call(kernel, out_shape=(jax.ShapeDtypeStruct((RANK, WIDTH // GR...]
    unnamed x2, local copies, waits for them, and re-layouts: 2.84 us -> 1.24 us
where the time goes in v2:
time: 60.4 us; the launch traced here: 60.2 us
  Pallas kernels  57.7 us (96%)
  between operations  1.29 us (2%)
  local copies, waits for them, and re-layouts  1.24 us (2%)
    pallas_call x1, Pallas kernels, on_device(): pl.pallas_call(kernel, out_shape=(jax.ShapeDtypeStruct((RANK, WIDTH // GR...  57.7 us
    unnamed x2, local copies, waits for them, and re-layouts  1.24 us

profile of v2, /device:TPU:6, one launch (start us, length us, event | category | flops | bytes accessed | tf_op | source)
XLA Modules:
  0.0 60.2 jit_solution(17042707979448784253)
XLA Ops:
  1.3 57.7 %shard_map.95 = (f32[32,320]{1,0:T(8,128)S(1)}, f32[32,384]{1,0:T(8,128)S(1)}) custom-call(bf16[128,2560]{1,0:T(8,128)(2,1)} %layer_hbm.1, bf16[1024,384]{1,0:T(8,128)(2,1)} %q_hbm.1, bf16[1024,384]{1,0:T(8,128)(2,1)} %k_hbm.1, bf16[1024,384]{1,0:T(8,128)(2,1)} %g_hbm.1, bf16[2560,384]{1,0:T(8,128)(2,1)} %feedback_hbm.1, f32[32,384]{1,0:T(8,128)} %factor_hbm.1, ...), custom_call_target="tpu_custom_call" | custom-call | tf_op jit(solution)/shard_map/pallas_call | solution.py:420
  59.0 0.6 %copy.13 = f32[32,320]{1,0:T(8,128)} copy(f32[32,320]{1,0:T(8,128)S(1)} %get-tuple-element.4) | data formatting | bytes 81920
  59.6 0.6 %copy.14 = f32[32,384]{1,0:T(8,128)} copy(f32[32,384]{1,0:T(8,128)S(1)} %get-tuple-element.5) | data formatting | bytes 98304

commit v3 on v2

--- a/solution.py
+++ b/solution.py
@@ -30,6 +30,7 @@
 BLOCK = 256
 BLOCKS = SLOTS // BLOCK
 MASKED = -1e30
+PENALTY = 65536.0
 
 
 def ahead(position, step, size):
@@ -57,69 +58,61 @@
 HOLDERS = [(xh, (xh + 2 * ch) % NY, ch) for ch in range(NC) for xh in range(NX)]
 
 
-def segment_starts(seg, count):
-    rows = lax.broadcasted_iota(jnp.int32, seg.shape, 0)
-    lanes = lax.broadcasted_iota(jnp.int32, seg.shape, 1)
-    slot = rows * LANES + lanes
-    wrapped = pltpu.roll(seg, 1, 1)
-    before = jnp.where(lanes == 0, pltpu.roll(wrapped, 1, 0), wrapped)
-    first = jnp.where((seg != before) & (slot > 0), slot, 0)
-    step = 1
-    while step < LANES:
-        first = jnp.maximum(first, jnp.where(lanes >= step, pltpu.roll(first, step, 1), 0))
-        step *= 2
-    carry = jnp.broadcast_to(jnp.max(first, axis=1, keepdims=True), first.shape)
-    step = 1
-    while step < SLOTS // LANES:
-        carry = jnp.maximum(carry, jnp.where(rows >= step, pltpu.roll(carry, step, 0), 0))
-        step *= 2
-    first = jnp.maximum(first, jnp.where(rows >= 1, pltpu.roll(carry, 1, 0), 0))
-    return jnp.where(slot < count, first, 4 * SLOTS)
-
-
 def split(value):
     high = value.astype(BF16)
     low = (value - high.astype(F32)).astype(BF16)
     return jnp.concatenate([high, low], axis=0)
 
 
-def attend(head, starts, k_ref, q_ref, g_ref, w_ref, v_ref):
+def document_columns(seg, key_ref, query_ref):
+    for b in range(SLOTS // LANES):
+        ids = lax.broadcasted_iota(jnp.int32, (LANES, LANES), 0)
+        own = jnp.where(seg[b:b + 1, :] == ids, 1.0, 0.0).T
+        key_ref[b * LANES:(b + 1) * LANES, :] = own.astype(BF16)
+        query_ref[b * LANES:(b + 1) * LANES, :] = ((own - 1.0) * PENALTY).astype(BF16)
+
+
+def scores(head, b, k_ref, q_ref, dk_ref, dq_ref):
     lanes = slice(head * HEAD_DIM, (head + 1) * HEAD_DIM)
+    low, high = b * BLOCK, (b + 1) * BLOCK
+    q = jnp.concatenate([q_ref[low:high, lanes], dq_ref[low:high, :]], axis=1)
+    k = jnp.concatenate([k_ref[low:high, lanes], dk_ref[low:high, :]], axis=1)
+    near = lax.dot_general(k, q, NT, preferred_element_type=F32)
+    key = lax.broadcasted_iota(jnp.int32, (BLOCK, BLOCK), 0)
+    query = lax.broadcasted_iota(jnp.int32, (BLOCK, BLOCK), 1)
+    near = jnp.where(key <= query, near, MASKED)
+    top = jnp.max(near, axis=0, keepdims=True)
+    parts = [near]
+    if b:
+        k = jnp.concatenate([k_ref[0:low, lanes], dk_ref[0:low, :]], axis=1)
+        far = lax.dot_general(k, q, NT, preferred_element_type=F32)
+        top = jnp.maximum(top, jnp.max(far, axis=0, keepdims=True))
+        parts.append(far)
+    return parts, top
+
+
+def weigh(b, count, parts, top, w_ref):
     rate = HEAD_DIM ** (-0.5) * math.log2(math.e)
-    for b in range(BLOCKS):
-        low, high = b * BLOCK, (b + 1) * BLOCK
-        q = q_ref[low:high, lanes]
-        start = starts[b]
-        live = start < SLOTS
-        key = lax.broadcasted_iota(jnp.int32, (BLOCK, BLOCK), 0) + low
-        query = lax.broadcasted_iota(jnp.int32, (BLOCK, BLOCK), 1) + low
-        near = lax.dot_general(k_ref[low:high, lanes], q, NT, preferred_element_type=F32)
-        near = jnp.where((key >= start) & (key <= query), near, MASKED)
-        top = jnp.max(near, axis=0, keepdims=True)
-        if b:
-            far = lax.dot_general(k_ref[0:low, lanes], q, NT, preferred_element_type=F32)
-            far_key = lax.broadcasted_iota(jnp.int32, (low, BLOCK), 0)
-            far = jnp.where(far_key >= start, far, MASKED)
-            top = jnp.maximum(top, jnp.max(far, axis=0, keepdims=True))
-        near = jnp.exp2((near - top) * rate)
-        total = jnp.sum(near, axis=0, keepdims=True)
-        if b:
-            far = jnp.exp2((far - top) * rate)
-            total = total + jnp.sum(far, axis=0, keepdims=True)
-        scale = jnp.where(live, 1.0 / jnp.maximum(total, 1.0), 0.0)
-        w_ref[low:high, low:high] = (near * scale).astype(BF16)
-        if b:
-            w_ref[0:low, low:high] = (far * scale).astype(BF16)
-    for b in range(BLOCKS):
-        low, high = b * BLOCK, (b + 1) * BLOCK
-        v = jnp.dot(w_ref[low:high, low:], g_ref[low:, lanes], preferred_element_type=F32)
-        v_ref[low:high, lanes] = v.astype(BF16)
+    low, high = b * BLOCK, (b + 1) * BLOCK
+    parts = [jnp.exp2((part - top) * rate) for part in parts]
+    total = sum(jnp.sum(part, axis=0, keepdims=True) for part in parts)
+    live = lax.broadcasted_iota(jnp.int32, (1, BLOCK), 1) + low < count
+    scale = jnp.where(live, 1.0 / jnp.maximum(total, 1.0), 0.0)
+    for part, (start, end) in zip(parts, ((low, high), (0, low))):
+        w_ref[start:end, low:high] = (part * scale).astype(BF16)
+
+
+def combine(head, b, g_ref, w_ref, v_ref):
+    lanes = slice(head * HEAD_DIM, (head + 1) * HEAD_DIM)
+    low, high = b * BLOCK, (b + 1) * BLOCK
+    v = jnp.dot(w_ref[low:high, low:], g_ref[low:, lanes], preferred_element_type=F32)
+    v_ref[low:high, lanes] = v.astype(BF16)
 
 
 def kernel(
     layer_hbm, q_hbm, k_hbm, g_hbm, feedback_hbm, factor_hbm, count_ref, segment_hbm,
     basis_ref, next_ref,
-    factor_ref, segment_ref,
+    factor_ref, segment_ref, dk_ref, dq_ref,
     q_ref, k_ref, g_ref, f_ref, l_ref, v_ref, w_ref, pf_ref,
     zs_ref, zr_ref, part_ref, main_ref, extra_ref, deep_ref, left_ref, t_ref, ys_ref, xr_ref, deep2_ref, yf_ref,
     load_sem,
@@ -169,14 +162,28 @@
         pltpu.make_async_copy(target, target, recv_sem).wait()
 
     arrived(segment_ref, load_sem.at[HEADS])
-    starts = segment_starts(segment_ref[...], count_ref[0])
+    document_columns(segment_ref[...], dk_ref, dq_ref)
     per = BLOCK // LANES
-    starts = [
-        jnp.concatenate([starts[b * per + i:b * per + i + 1] for i in range(per)], axis=1) for b in range(BLOCKS)
-    ]
-    for head in range(HEADS):
-        arrived(k_ref, load_sem.at[head])
-        attend(head, starts, k_ref, q_ref, g_ref, w_ref.at[head], v_ref)
+    units = [(head, b) for b in reversed(range(BLOCKS)) for head in range(HEADS)]
+
+    def begin(unit):
+        head, b = units[unit]
+        if b == BLOCKS - 1:
+            arrived(k_ref, load_sem.at[head])
+        return scores(head, b, k_ref, q_ref, dk_ref, dq_ref)
+
+    ready = [begin(unit) for unit in range(1)]
+    waiting = []
+    for unit, (head, b) in enumerate(units):
+        if unit + 1 < len(units):
+            ready.append(begin(unit + 1))
+        weigh(b, count_ref[0], *ready.pop(0), w_ref.at[head])
+        waiting.append((head, b))
+        if len(waiting) > 1:
+            last, block = waiting.pop(0)
+            combine(last, block, g_ref, w_ref.at[last], v_ref)
+    for last, block in waiting:
+        combine(last, block, g_ref, w_ref.at[last], v_ref)
 
     arrived(factor_ref, load_sem.at[HEADS + 1])
     factor = split(factor_ref[...])
@@ -267,9 +274,17 @@
         for where in plane_device:
             send(left_ref.at[spare], left_ref.at[spare], ag_send.at[1], ag_recv.at[1], where)
 
+    def columns(first, last):
+        return jnp.concatenate(
+            [jnp.concatenate([left_ref[h * TILES + n] for h in range(NC)], axis=0) for n in range(first, last)], axis=1
+        )
+
     drain_depth()
     arrived(left_ref.at[pl.ds(0, OTHERS)], ag_recv.at[0])
 
+    left = columns(0, MAIN)
+    product = lax.dot_general(left, l_ref[:, :MAIN * LANES], NT, preferred_element_type=F32)
+
     @pl.when(holder)
     def _():
         arrived(left_ref.at[pl.ds(0, len(HOLDERS) - 1)], ag_recv.at[1])
@@ -277,6 +292,11 @@
     @pl.when(jnp.logical_not(holder))
     def _():
         arrived(left_ref.at[pl.ds(0, len(HOLDERS))], ag_recv.at[1])
+
+    rest = columns(MAIN, TILES)
+    product = product + lax.dot_general(rest, l_ref[:, MAIN * LANES:], NT, preferred_element_type=F32)
+    left = jnp.concatenate([left, rest], axis=1)
+    t_ref[tp] = product.astype(BF16)
 
     def drain_gather():
         arrived(left_ref.at[pl.ds(0, OTHERS)], ag_send.at[0])
@@ -285,11 +305,6 @@
         def _():
             arrived(left_ref.at[pl.ds(0, OTHERS)], ag_send.at[1])
 
-
-    left = jnp.concatenate(
-        [jnp.concatenate([left_ref[h * TILES + n] for h in range(NC)], axis=0) for n in range(TILES)], axis=1
-    )
-    t_ref[tp] = lax.dot_general(left, l_ref[...], NT, preferred_element_type=F32).astype(BF16)
     for step in GROUP_STEPS:
         px, py, pc = plane_peer(step)
         send(t_ref.at[tp], t_ref.at[tp], t_send, t_recv, (dp, py * NC + pc))
@@ -297,21 +312,27 @@
     drain_gather()
     arrived(t_ref.at[pl.ds(0, GROUP - 1)], t_recv)
     gathered = jnp.concatenate([t_ref[t] for t in range(GROUP)], axis=1)
-    right = right + jnp.dot(gathered, v_ref[...], preferred_element_type=F32)
-
-    for j in range(FEATURES // LANES):
-        for h in range(NC):
-            ys_ref[j * NC + h] = right[h * HALF:(h + 1) * HALF, j * LANES:(j + 1) * LANES]
+
     keeper = x // 2 == c
     odd = NX + x % 2
     row_device = [device(ahead(x, step, NX), y, c, z) for step in ROW_STEPS]
-    for step, where in zip(ROW_STEPS, row_device):
-        send(ys_ref.at[ahead(x, step, NX)], xr_ref.at[0, x], x_send.at[0], x_recv.at[0], where)
-    for e in range(2):
-
-        @pl.when(x != 2 * c + e)
-        def _():
-            send(ys_ref.at[NX + e], xr_ref.at[1, x], x_send.at[1 + e], x_recv.at[1], device(2 * c + e, y, c, z))
+    for j in range(FEATURES // LANES):
+        lanes = slice(j * LANES, (j + 1) * LANES)
+        got = right[:, lanes] + jnp.dot(gathered, v_ref[:, lanes], preferred_element_type=F32)
+        for h in range(NC):
+            tile = j * NC + h
+            ys_ref[tile] = got[h * HALF:(h + 1) * HALF]
+            if tile < NX:
+
+                @pl.when(x != tile)
+                def _():
+                    send(ys_ref.at[tile], xr_ref.at[0, x], x_send.at[0], x_recv.at[0], device(tile, y, c, z))
+            else:
+                taker = 2 * c + tile - NX
+
+                @pl.when(x != taker)
+                def _():
+                    send(ys_ref.at[tile], xr_ref.at[1, x], x_send.at[1 + tile - NX], x_recv.at[1], device(taker, y, c, z))
 
     xr_ref[0, x] = ys_ref[x]
     xr_ref[1, x] = ys_ref[odd]
@@ -350,16 +371,23 @@
     pivots = jnp.sum(jnp.where(lanes == rows, table, 0.0), axis=1, keepdims=True)
     inverse = jnp.where(lanes >= RANK, table, 0.0) * lax.rsqrt(pivots)
 
+    inverse = split(inverse)
+
+    def padded(value):
+        above, below = jnp.zeros((RANK, FEATURES), BF16), jnp.zeros((LANES - 2 * RANK, FEATURES), BF16)
+        return jnp.concatenate([above, value, below], axis=0)
+
     def solve(value):
-        padded = jnp.concatenate(
-            [jnp.zeros((RANK, FEATURES), F32), value, jnp.zeros((LANES - 2 * RANK, FEATURES), F32)], axis=0
-        )
-        return jnp.dot(inverse, padded, precision=lax.Precision.HIGHEST, preferred_element_type=F32)
+        pieces = [value] if value.dtype == BF16 else [value.astype(BF16)]
+        if value.dtype == F32:
+            pieces.append((value - pieces[0].astype(F32)).astype(BF16))
+        terms = [jnp.dot(inverse, padded(piece), preferred_element_type=F32) for piece in pieces]
+        return sum(term[:RANK] + term[RANK:] for term in reversed(terms))
 
     first = (5 * tp) // 2
     window = jnp.concatenate(
         [
-            jnp.concatenate([left_ref[h * TILES + first + i] for h in range(NC)], axis=0).astype(F32)
+            jnp.concatenate([left_ref[h * TILES + first + i] for h in range(NC)], axis=0)
             for i in range(FEATURES // LANES)
         ],
         axis=1,
@@ -411,13 +439,18 @@
         arrived(yf_ref.at[pl.ds(0, NX - 1)], xg_send.at[1])
 
 
+def place_results(basis_ref, factor_ref, basis_out, factor_out):
+    basis_out[...] = basis_ref[...]
+    factor_out[...] = factor_ref[...]
+
+
 def on_device(
     layer_input, queries, key_vectors, out_grad, feedback, factor_prev, token_count, segment_ids
 ):
     vmem = pl.BlockSpec(memory_space=pltpu.VMEM)
     anywhere = pl.BlockSpec(memory_space=pltpu.HBM)
     dma = pltpu.SemaphoreType.DMA
-    return pl.pallas_call(
+    basis, factor = pl.pallas_call(
         kernel,
         out_shape=(
             jax.ShapeDtypeStruct((RANK, WIDTH // GROUP), F32),
@@ -428,6 +461,8 @@
         scratch_shapes=[
             pltpu.VMEM((RANK, FEATURES), F32),
             pltpu.VMEM((SLOTS // LANES, LANES), jnp.int32),
+            pltpu.VMEM((SLOTS, LANES), BF16),
+            pltpu.VMEM((SLOTS, LANES), BF16),
             pltpu.VMEM((SLOTS, FEATURES), BF16),
             pltpu.VMEM((SLOTS, FEATURES), BF16),
             pltpu.VMEM((SLOTS, FEATURES), BF16),
@@ -469,6 +504,16 @@
         token_count,
         pltpu.with_memory_space_constraint(segment_ids.reshape(SLOTS // LANES, LANES), pltpu.HBM),
     )
+    return pl.pallas_call(
+        place_results,
+        out_shape=(
+            jax.ShapeDtypeStruct((RANK, WIDTH // GROUP), F32),
+            jax.ShapeDtypeStruct((RANK, FEATURES), F32),
+        ),
+        in_specs=[vmem, vmem],
+        out_specs=(vmem, vmem),
+        compiler_params=pltpu.CompilerParams(vmem_limit_bytes=4 * 1024 * 1024),
+    )(basis, factor)
 
 
 def solution(mesh):

time: 60.4 us -> 60.3 us (level)
  local copies, waits for them, and re-layouts: 1.24 us -> 0 us
  Pallas kernels: 57.7 us -> 58.8 us
    unnamed x2 -> x0, local copies, waits for them, and re-layouts: 1.24 us -> none
    pallas_call x0 -> x1, Pallas kernels: none -> 0.64 us  [on_device(): pl.pallas_call(place_results, out_shape=(jax.ShapeDtypeStruct((RANK, WIDT...]
where the time goes in v3:
time: 60.3 us; the launch traced here: 60.1 us
  Pallas kernels  58.8 us (98%)
  between operations  1.29 us (2%)
    pallas_call x1, Pallas kernels, on_device(): pl.pallas_call(kernel, out_shape=(jax.ShapeDtypeStruct((RANK, WIDTH // GR...  58.2 us

profile of v3, /device:TPU:6, one launch (start us, length us, event | category | flops | bytes accessed | tf_op | source)
XLA Modules:
  0.0 60.1 jit_solution(12798495573693688360)
XLA Ops:
  1.3 58.2 %shard_map.95 = (f32[32,320]{1,0:T(8,128)S(1)}, f32[32,384]{1,0:T(8,128)S(1)}) custom-call(bf16[128,2560]{1,0:T(8,128)(2,1)} %layer_hbm.1, bf16[1024,384]{1,0:T(8,128)(2,1)} %q_hbm.1, bf16[1024,384]{1,0:T(8,128)(2,1)} %k_hbm.1, bf16[1024,384]{1,0:T(8,128)(2,1)} %g_hbm.1, bf16[2560,384]{1,0:T(8,128)(2,1)} %feedback_hbm.1, f32[32,384]{1,0:T(8,128)} %factor_hbm.1, ...), custom_call_target="tpu_custom_call" | custom-call | tf_op jit(solution)/shard_map/pallas_call | solution.py:453
  59.5 0.6 %shard_map.96 = (f32[32,320]{1,0:T(8,128)}, f32[32,384]{1,0:T(8,128)}) custom-call(f32[32,320]{1,0:T(8,128)S(1)} %get-tuple-element.4.basis_ref, f32[32,384]{1,0:T(8,128)S(1)} %get-tuple-element.5.factor_ref), custom_call_target="tpu_custom_call" | custom-call | tf_op jit(solution)/shard_map/pallas_call | solution.py:507

commit v4 on v3

--- a/solution.py
+++ b/solution.py
@@ -16,6 +16,7 @@
 PLANE = NX * GROUP
 OTHERS = PLANE - 1
 DEEP = NZ - 1
+FAR = 7
 
 HEAD_DIM = 128
 HEADS = 3
@@ -139,13 +140,13 @@
         for source, target in ((k_hbm, k_ref), (q_hbm, q_ref), (g_hbm, g_ref)):
             load(source.at[:, lanes], target.at[:, lanes], head)
 
-    load(segment_hbm, segment_ref, HEADS)
-    load_head(0)
     barrier = pltpu.get_barrier_semaphore()
     for step in DEPTH_STEPS:
         pl.semaphore_signal(barrier, inc=1, device_id=device(x, y, c, ahead(z, step, NZ)), device_id_type=MESH)
     for step in PLANE_STEPS:
         pl.semaphore_signal(barrier, inc=1, device_id=device(*plane_peer(step), z), device_id_type=MESH)
+    load(segment_hbm, segment_ref, HEADS)
+    load_head(0)
     for head in range(1, HEADS):
         load_head(head)
     load(factor_hbm, factor_ref, HEADS + 1)
@@ -216,14 +217,15 @@
     holder = y == (x + 2 * c) % NY
     own = c * TILES + NY * x + y
     spare = c * TILES + MAIN + x
+    for xh, yh, ch in HOLDERS:
+
+        @pl.when(place != xh * GROUP + yh * NC + ch)
+        def _():
+            send(part_ref.at[ch * TILES + MAIN + xh], extra_ref.at[place], rs_send.at[1], rs_recv.at[1], device(xh, yh, ch, z))
+
     for step in PLANE_STEPS:
         px, py, pc = plane_peer(step)
         send(part_ref.at[pc * TILES + NY * px + py], main_ref.at[place], rs_send.at[0], rs_recv.at[0], device(px, py, pc, z))
-    for xh, yh, ch in HOLDERS:
-
-        @pl.when(place != xh * GROUP + yh * NC + ch)
-        def _():
-            send(part_ref.at[ch * TILES + MAIN + xh], extra_ref.at[place], rs_send.at[1], rs_recv.at[1], device(xh, yh, ch, z))
 
     main_ref[place] = part_ref[own]
     extra_ref[place] = part_ref[spare]
@@ -242,14 +244,22 @@
             arrived(part_ref.at[pl.ds(0, len(HOLDERS))], rs_send.at[1])
 
     deep_device = [device(x, y, c, ahead(z, step, NZ)) for step in DEPTH_STEPS]
-    for where in deep_device:
+    for where in deep_device[:FAR]:
         send(deep_ref.at[0, z], deep_ref.at[0, z], d_send.at[0], d_recv.at[0], where)
 
     @pl.when(holder)
     def _():
         arrived(extra_ref.at[pl.ds(0, OTHERS)], rs_recv.at[1])
         deep_ref[1, z] = jnp.sum(extra_ref[...].astype(F32), axis=0).astype(BF16)
-        for where in deep_device:
+        for where in deep_device[:FAR]:
+            send(deep_ref.at[1, z], deep_ref.at[1, z], d_send.at[1], d_recv.at[1], where)
+
+    for where in deep_device[FAR:]:
+        send(deep_ref.at[0, z], deep_ref.at[0, z], d_send.at[0], d_recv.at[0], where)
+
+    @pl.when(holder)
+    def _():
+        for where in deep_device[FAR:]:
             send(deep_ref.at[1, z], deep_ref.at[1, z], d_send.at[1], d_recv.at[1], where)
 
     drain_scatter()
@@ -348,14 +358,22 @@
             def _():
                 arrived(ys_ref.at[NX + e], x_send.at[1 + e])
 
-    for where in deep_device:
+    for where in deep_device[:FAR]:
         send(deep2_ref.at[0, z], deep2_ref.at[0, z], d2_send.at[0], d2_recv.at[0], where)
 
     @pl.when(keeper)
     def _():
         arrived(xr_ref.at[1, pl.ds(0, NX - 1)], x_recv.at[1])
         deep2_ref[1, z] = jnp.sum(xr_ref[1], axis=0).astype(BF16)
-        for where in deep_device:
+        for where in deep_device[:FAR]:
+            send(deep2_ref.at[1, z], deep2_ref.at[1, z], d2_send.at[1], d2_recv.at[1], where)
+
+    for where in deep_device[FAR:]:
+        send(deep2_ref.at[0, z], deep2_ref.at[0, z], d2_send.at[0], d2_recv.at[0], where)
+
+    @pl.when(keeper)
+    def _():
+        for where in deep_device[FAR:]:
             send(deep2_ref.at[1, z], deep2_ref.at[1, z], d2_send.at[1], d2_recv.at[1], where)
 
     drain_rows()

time: 60.3 us -> 59.1 us (0.980); the launches traced: 60.1 us -> 58.2 us
  Pallas kernels: 58.8 us -> 57 us
    pallas_call x1, Pallas kernels: 58.2 us -> 56.3 us  [on_device(): pl.pallas_call(kernel, out_shape=(jax.ShapeDtypeStruct((RANK, WIDTH // GR...]
where the time goes in v4:
time: 59.1 us; the launch traced here: 58.2 us
  Pallas kernels  57 us (96%)
  between operations  1.29 us (2%)
    pallas_call x1, Pallas kernels, on_device(): pl.pallas_call(kernel, out_shape=(jax.ShapeDtypeStruct((RANK, WIDTH // GR...  56.3 us

profile of v4, /device:TPU:6, one launch (start us, length us, event | category | flops | bytes accessed | tf_op | source)
XLA Modules:
  0.0 58.2 jit_solution(16160265054108950976)
XLA Ops:
  1.3 56.3 %shard_map.95 = (f32[32,320]{1,0:T(8,128)S(1)}, f32[32,384]{1,0:T(8,128)S(1)}) custom-call(bf16[128,2560]{1,0:T(8,128)(2,1)} %layer_hbm.1, bf16[1024,384]{1,0:T(8,128)(2,1)} %q_hbm.1, bf16[1024,384]{1,0:T(8,128)(2,1)} %k_hbm.1, bf16[1024,384]{1,0:T(8,128)(2,1)} %g_hbm.1, bf16[2560,384]{1,0:T(8,128)(2,1)} %feedback_hbm.1, f32[32,384]{1,0:T(8,128)} %factor_hbm.1, ...), custom_call_target="tpu_custom_call" | custom-call | tf_op jit(solution)/shard_map/pallas_call | solution.py:471
  57.6 0.6 %shard_map.96 = (f32[32,320]{1,0:T(8,128)}, f32[32,384]{1,0:T(8,128)}) custom-call(f32[32,320]{1,0:T(8,128)S(1)} %get-tuple-element.4.basis_ref, f32[32,384]{1,0:T(8,128)S(1)} %get-tuple-element.5.factor_ref), custom_call_target="tpu_custom_call" | custom-call | tf_op jit(solution)/shard_map/pallas_call | solution.py:525

commit v5 on v4

--- a/solution.py
+++ b/solution.py
@@ -143,10 +143,10 @@
     barrier = pltpu.get_barrier_semaphore()
     for step in DEPTH_STEPS:
         pl.semaphore_signal(barrier, inc=1, device_id=device(x, y, c, ahead(z, step, NZ)), device_id_type=MESH)
+    load(segment_hbm, segment_ref, HEADS)
+    load_head(0)
     for step in PLANE_STEPS:
         pl.semaphore_signal(barrier, inc=1, device_id=device(*plane_peer(step), z), device_id_type=MESH)
-    load(segment_hbm, segment_ref, HEADS)
-    load_head(0)
     for head in range(1, HEADS):
         load_head(head)
     load(factor_hbm, factor_ref, HEADS + 1)
@@ -203,7 +203,6 @@
         got = lax.dot_general(factor, f_ref[j * BLOCK:(j + 1) * BLOCK, :], NT, preferred_element_type=F32)
         pf_ref[:, j * BLOCK:(j + 1) * BLOCK] = got[:RANK] + got[RANK:]
     arrived(l_ref, load_sem.at[HEADS + 3])
-    arrived(zs_ref.at[pl.ds(0, GROUP - 1)], a_send)
     arrived(zr_ref.at[pl.ds(0, GROUP - 1)], a_recv)
     mixed = split(jnp.sum(zr_ref[...], axis=0))
     for j in range(WIDTH // BLOCK):
@@ -262,7 +261,6 @@
         for where in deep_device[FAR:]:
             send(deep_ref.at[1, z], deep_ref.at[1, z], d_send.at[1], d_recv.at[1], where)
 
-    drain_scatter()
     arrived(deep_ref.at[0, pl.ds(0, DEEP)], d_recv.at[0])
     left_ref[own] = jnp.sum(deep_ref[0].astype(F32), axis=0).astype(BF16)
 
@@ -289,7 +287,6 @@
             [jnp.concatenate([left_ref[h * TILES + n] for h in range(NC)], axis=0) for n in range(first, last)], axis=1
         )
 
-    drain_depth()
     arrived(left_ref.at[pl.ds(0, OTHERS)], ag_recv.at[0])
 
     left = columns(0, MAIN)
@@ -319,14 +316,13 @@
         px, py, pc = plane_peer(step)
         send(t_ref.at[tp], t_ref.at[tp], t_send, t_recv, (dp, py * NC + pc))
     right = jnp.dot(left, f_ref[...], preferred_element_type=F32)
-    drain_gather()
     arrived(t_ref.at[pl.ds(0, GROUP - 1)], t_recv)
     gathered = jnp.concatenate([t_ref[t] for t in range(GROUP)], axis=1)
 
     keeper = x // 2 == c
     odd = NX + x % 2
     row_device = [device(ahead(x, step, NX), y, c, z) for step in ROW_STEPS]
-    for j in range(FEATURES // LANES):
+    for j in reversed(range(FEATURES // LANES)):
         lanes = slice(j * LANES, (j + 1) * LANES)
         got = right[:, lanes] + jnp.dot(gathered, v_ref[:, lanes], preferred_element_type=F32)
         for h in range(NC):
@@ -376,7 +372,10 @@
         for where in deep_device[FAR:]:
             send(deep2_ref.at[1, z], deep2_ref.at[1, z], d2_send.at[1], d2_recv.at[1], where)
 
-    drain_rows()
+    arrived(zs_ref.at[pl.ds(0, GROUP - 1)], a_send)
+    drain_scatter()
+    drain_depth()
+    drain_gather()
 
     tall = jnp.concatenate([left, jnp.zeros((LANES - RANK, WIDTH), BF16)], axis=0)
     table = lax.dot_general(left, tall, NT, preferred_element_type=F32)
@@ -434,7 +433,6 @@
         for where in row_device:
             send(yf_ref.at[odd], yf_ref.at[odd], xg_send.at[1], xg_recv.at[1 + x % 2], where)
 
-    drain_depth2()
     arrived(yf_ref.at[pl.ds(0, NX - 1)], xg_recv.at[0])
     for e in range(2):
 
@@ -450,6 +448,8 @@
         axis=1,
     )
     next_ref[...] = solve(summed) * (1.0 / (NX * NZ))
+    drain_rows()
+    drain_depth2()
     arrived(yf_ref.at[pl.ds(0, NX - 1)], xg_send.at[0])
 
     @pl.when(keeper)

time: 59.1 us -> 59.2 us (level)
  no operation moved by 1% of the time
where the time goes in v5:
time: 59.2 us; the launch traced here: 58.5 us
  Pallas kernels  57.2 us (97%)
  between operations  1.29 us (2%)
    pallas_call x1, Pallas kernels, on_device(): pl.pallas_call(kernel, out_shape=(jax.ShapeDtypeStruct((RANK, WIDTH // GR...  56.5 us

profile of v5, /device:TPU:6, one launch (start us, length us, event | category | flops | bytes accessed | tf_op | source)
XLA Modules:
  0.0 58.5 jit_solution(3744260894756517962)
XLA Ops:
  1.3 56.5 %shard_map.95 = (f32[32,320]{1,0:T(8,128)S(1)}, f32[32,384]{1,0:T(8,128)S(1)}) custom-call(bf16[128,2560]{1,0:T(8,128)(2,1)} %layer_hbm.1, bf16[1024,384]{1,0:T(8,128)(2,1)} %q_hbm.1, bf16[1024,384]{1,0:T(8,128)(2,1)} %k_hbm.1, bf16[1024,384]{1,0:T(8,128)(2,1)} %g_hbm.1, bf16[2560,384]{1,0:T(8,128)(2,1)} %feedback_hbm.1, f32[32,384]{1,0:T(8,128)} %factor_hbm.1, ...), custom_call_target="tpu_custom_call" | custom-call | tf_op jit(solution)/shard_map/pallas_call | solution.py:471
  57.8 0.6 %shard_map.96 = (f32[32,320]{1,0:T(8,128)}, f32[32,384]{1,0:T(8,128)}) custom-call(f32[32,320]{1,0:T(8,128)S(1)} %get-tuple-element.4.basis_ref, f32[32,384]{1,0:T(8,128)S(1)} %get-tuple-element.5.factor_ref), custom_call_target="tpu_custom_call" | custom-call | tf_op jit(solution)/shard_map/pallas_call | solution.py:525

commit v6 on v5

--- a/solution.py
+++ b/solution.py
@@ -190,7 +190,7 @@
     factor = split(factor_ref[...])
     for t in range(GROUP):
         got = lax.dot_general(factor, v_ref[t * LANES:(t + 1) * LANES, :], NT, preferred_element_type=F32)
-        zs_ref[t] = got[:RANK] + got[RANK:]
+        zs_ref[t] = (got[:RANK] + got[RANK:]).astype(BF16)
     pl.semaphore_wait(barrier, len(DEPTH_STEPS) + len(PLANE_STEPS))
     for step in GROUP_STEPS:
         px, py, pc = plane_peer(step)
@@ -204,7 +204,7 @@
         pf_ref[:, j * BLOCK:(j + 1) * BLOCK] = got[:RANK] + got[RANK:]
     arrived(l_ref, load_sem.at[HEADS + 3])
     arrived(zr_ref.at[pl.ds(0, GROUP - 1)], a_recv)
-    mixed = split(jnp.sum(zr_ref[...], axis=0))
+    mixed = split(jnp.sum(zr_ref[...].astype(F32), axis=0))
     for j in range(WIDTH // BLOCK):
         lanes = slice(j * BLOCK, (j + 1) * BLOCK)
         got = jnp.dot(mixed, l_ref[:, lanes], preferred_element_type=F32)
@@ -489,8 +489,8 @@
             pltpu.VMEM((SLOTS, FEATURES), BF16),
             pltpu.VMEM((HEADS, SLOTS, SLOTS), BF16),
             pltpu.VMEM((RANK, WIDTH), F32),
-            pltpu.VMEM((GROUP, RANK, LANES), F32),
-            pltpu.VMEM((GROUP, RANK, LANES), F32),
+            pltpu.VMEM((GROUP, RANK, LANES), BF16),
+            pltpu.VMEM((GROUP, RANK, LANES), BF16),
             pltpu.VMEM((NC * TILES, HALF, LANES), BF16),
             pltpu.VMEM((PLANE, HALF, LANES), BF16),
             pltpu.VMEM((PLANE, HALF, LANES), BF16),

time: 59.2 us -> 58.5 us (0.988)
  no operation moved by 1% of the time
where the time goes in v6:
time: 58.5 us; the launch traced here: 58.3 us
  Pallas kernels  57 us (97%)
  between operations  1.29 us (2%)
    pallas_call x1, Pallas kernels, on_device(): pl.pallas_call(kernel, out_shape=(jax.ShapeDtypeStruct((RANK, WIDTH // GR...  56.4 us

profile of v6, /device:TPU:6, one launch (start us, length us, event | category | flops | bytes accessed | tf_op | source)
XLA Modules:
  0.0 58.3 jit_solution(15579110915198911158)
XLA Ops:
  1.3 56.4 %shard_map.95 = (f32[32,320]{1,0:T(8,128)S(1)}, f32[32,384]{1,0:T(8,128)S(1)}) custom-call(bf16[128,2560]{1,0:T(8,128)(2,1)} %layer_hbm.1, bf16[1024,384]{1,0:T(8,128)(2,1)} %q_hbm.1, bf16[1024,384]{1,0:T(8,128)(2,1)} %k_hbm.1, bf16[1024,384]{1,0:T(8,128)(2,1)} %g_hbm.1, bf16[2560,384]{1,0:T(8,128)(2,1)} %feedback_hbm.1, f32[32,384]{1,0:T(8,128)} %factor_hbm.1, ...), custom_call_target="tpu_custom_call" | custom-call | tf_op jit(solution)/shard_map/pallas_call | solution.py:471
  57.6 0.6 %shard_map.96 = (f32[32,320]{1,0:T(8,128)}, f32[32,384]{1,0:T(8,128)}) custom-call(f32[32,320]{1,0:T(8,128)S(1)} %get-tuple-element.4.basis_ref, f32[32,384]{1,0:T(8,128)S(1)} %get-tuple-element.5.factor_ref), custom_call_target="tpu_custom_call" | custom-call | tf_op jit(solution)/shard_map/pallas_call | solution.py:525
